TPU v7x, 256 devices: a whole 4x4x8 slice. The times are simulated.
256 devices in a mesh: cells: 32 (over y, z), modes: 8 (over x, core).
Axes of the slice: x: 4, y: 4, z: 8, core: 2. Of those that a mesh axis runs over, the one named last changes fastest.
Arguments:
- adjoint_source: float32 [128, 65536], P('modes', 'cells'), may hold values from -6 to 6
- coupling: float32 [9, 128, 128], replicated, may hold values from -0.5 to 0.5
- diag_blocks: bfloat16 [512, 9, 128, 128], P(('cells', 'modes')), may hold values from -0.125 to 0.125
- off_blocks: bfloat16 [512, 9, 128, 128], P(('cells', 'modes')), may hold values from -0.125 to 0.125
- owner_cells: int32 [512, 9, 1], P(('cells', 'modes')), may hold values from 0 to 31; in each aligned block of 18 rows (0 to 17, 18 to 35, ..., all dimensions but the last counted through in order) no two rows name the same one
- target_block: int32 [512, 9], P(('cells', 'modes')), may hold values from 0 to 15
Outputs:
- solution: float32 [128, 65536], P('modes', 'cells')
- next_basis: float32 [128, 65536], P('modes', 'cells')
Inputs may be any that keep to these rules, and one draw needn't show every extreme that they name: `owner_cells`: among the 18 off-diagonal blocks of the rows of one device, at most 1 name the same owner, and in every draw some device's rows name some owner exactly 1 times.
All inputs are finite; a program needn't handle non-finite values.
Results may differ from a plain program's by a relative error of at most 0.004.
Values sent between devices are 32-bit elements; how exact they have to be, the bound alone decides.
A program may use at most 64 MiB of HBM per device.

v0:
```python
import jax
import jax.numpy as jnp
from jax import lax
from jax.sharding import PartitionSpec as P

ITERS = 2


def transposed_apply(vector_in, coupling, diag_blocks, off_blocks, owner_cells, target_block):
    modes_total = coupling.shape[1]
    blocks_here = diag_blocks.shape[0]
    term_count = diag_blocks.shape[1]
    block_width = diag_blocks.shape[2]
    cell_groups = lax.axis_size("cells")
    mode_groups = lax.axis_size("modes")
    mode_rows = modes_total // mode_groups
    slab_blocks = mode_groups * blocks_here
    entries = term_count * blocks_here
    slot_count = (entries + cell_groups - 1) // cell_groups
    regrouped = lax.all_to_all(vector_in, "modes", split_axis=1, concat_axis=0, tiled=True).reshape(
        modes_total, blocks_here, block_width
    )
    mixed_modes = jnp.einsum(
        "kpq,pbc->kqbc",
        coupling,
        regrouped,
        precision=lax.Precision.HIGHEST,
        preferred_element_type=jnp.float32,
    ).astype(jnp.bfloat16)
    near_terms = jnp.einsum(
        "kqbc,bkcd->qbd", mixed_modes, diag_blocks, preferred_element_type=jnp.float32
    )
    far_terms = jnp.einsum(
        "kqbc,bkcd->bkqd", mixed_modes, off_blocks, preferred_element_type=jnp.float32
    )
    far_terms = far_terms.reshape(entries, modes_total, block_width)
    owners = owner_cells.reshape(entries)
    same_owner = owners[:, None] == owners[None, :]
    order_idx = jnp.arange(entries, dtype=jnp.int32)
    earlier = order_idx[:, None] > order_idx[None, :]
    slot_rank = jnp.sum(jnp.logical_and(same_owner, earlier), axis=1)
    position = owners * slot_count + slot_rank
    outgoing = (
        jnp.zeros((cell_groups * slot_count, modes_total, block_width), jnp.float32)
        .at[position]
        .set(far_terms)
    )
    outgoing = outgoing.reshape(cell_groups, slot_count, modes_total, block_width)
    labels = (
        jnp.full((cell_groups * slot_count,), slab_blocks, jnp.int32)
        .at[position]
        .set(target_block.reshape(entries))
    )
    labels = jnp.broadcast_to(
        labels.reshape(cell_groups, slot_count, 1), (cell_groups, slot_count, mode_groups)
    )
    arrived, arrived_labels = (
        lax.all_to_all(
            lax.all_to_all(outgoing, "cells", split_axis=0, concat_axis=0, tiled=True),
            "modes",
            split_axis=2,
            concat_axis=1,
            tiled=True,
        ),
        lax.all_to_all(
            lax.all_to_all(labels, "cells", split_axis=0, concat_axis=0, tiled=True),
            "modes",
            split_axis=2,
            concat_axis=1,
            tiled=True,
        ),
    )
    collected = jax.ops.segment_sum(
        arrived.reshape(-1, mode_rows, block_width),
        arrived_labels.reshape(-1),
        num_segments=slab_blocks + 1,
    )[:slab_blocks]
    returned = lax.all_to_all(
        near_terms.reshape(modes_total, blocks_here * block_width),
        "modes",
        split_axis=0,
        concat_axis=1,
        tiled=True,
    )
    return returned + collected.transpose(1, 0, 2).reshape(mode_rows, slab_blocks * block_width)


def solve_small(columns, source_size):
    column_count = len(columns)
    rhs_terms = [source_size] + [source_size * 0.0 for unused in range(column_count)]
    cosines = []
    sine_list = []
    upper_cols = []
    for current in range(column_count):
        column = list(columns[current])
        for previous in range(current):
            first_val = column[previous]
            second_val = column[previous + 1]
            column[previous] = cosines[previous] * first_val + sine_list[previous] * second_val
            column[previous + 1] = cosines[previous] * second_val - sine_list[previous] * first_val
        radius = jnp.sqrt(
            column[current] * column[current] + column[current + 1] * column[current + 1]
        )
        cosine = column[current] / radius
        sine_val = column[current + 1] / radius
        column[current] = radius
        rhs_terms[current + 1] = -sine_val * rhs_terms[current]
        rhs_terms[current] = cosine * rhs_terms[current]
        cosines.append(cosine)
        sine_list.append(sine_val)
        upper_cols.append(column)
    weights = [source_size] * column_count
    for current in reversed(range(column_count)):
        residue = rhs_terms[current]
        for later_idx in range(current + 1, column_count):
            residue = residue - upper_cols[later_idx][current] * weights[later_idx]
        weights[current] = residue / upper_cols[current][current]
    return weights


def body(adjoint_source, coupling, diag_blocks, off_blocks, owner_cells, target_block):
    source_size = jnp.sqrt(lax.psum(jnp.sum(adjoint_source * adjoint_source), ("cells", "modes")))
    basis = [adjoint_source / source_size]
    columns = []
    for current in range(ITERS):
        candidate = transposed_apply(
            basis[current], coupling, diag_blocks, off_blocks, owner_cells, target_block
        )
        heights = []
        for vector in basis:
            product = lax.psum(jnp.sum(candidate * vector), ("cells", "modes"))
            candidate = candidate - product * vector
            heights.append(product)
        length = jnp.sqrt(lax.psum(jnp.sum(candidate * candidate), ("cells", "modes")))
        heights.append(length)
        columns.append(heights)
        basis.append(candidate / length)
    weights = solve_small(columns, source_size)
    solution = weights[0] * basis[0]
    current = 1
    solution = solution + weights[current] * basis[current]
    return (solution, source_size * basis[ITERS])


def solution(mesh):
    placed = (
        P("modes", "cells"),
        P(),
        P(("cells", "modes"), None, None, None),
        P(("cells", "modes"), None, None, None),
        P(("cells", "modes"), None, None),
        P(("cells", "modes"), None),
    )
    return jax.shard_map(
        body,
        mesh=mesh,
        in_specs=placed,
        out_specs=(P("modes", "cells"), P("modes", "cells")),
        check_vma=False,
    )
```

profile of v0, /device:TPU:1, one launch (start us, length us, event | category | flops | bytes accessed | tf_op | source)
XLA Modules:
  0.0 759.5 jit_solution(9016287767804324863)
XLA Ops:
  7.3 12.0 %all-to-all-start.2 = ((s32[32,1,8]{2,1,0:T(1,128)}), s32[32,1,8]{2,1,0:T(1,128)S(1)}, u32[]{:S(2)}, u32[]{:S(2)}) async-start(s32[32,1,8]{2,1,0:T(1,128)} %broadcast_in_dim.2), calls=%async_computation.2 | async-start | bytes 32768 | tf_op jit(solution)/shard_map/all_to_all | solution.py:66
  19.3 77.2 %psum.42 = f32[]{:T(128)} all-reduce(f32[]{:T(128)} %multiply_reduce_fusion.5), channel_id=1, replica_groups=mesh['cells'=32,'modes'=8] {'cells','modes'}, use_global_device_ids=true, to_apply=%region_1.0 | all-reduce | flops 1 | bytes 8 | tf_op jit(solution)/shard_map/psum | solution.py:122
  103.4 4.6 all-to-all-done
  108.0 4.1 all-to-all-start.3
  115.3 5.6 scatter_fusion
  120.9 6.8 all-to-all-start.4
  130.0 46.8 %all-to-all-done.4 = f32[32,1,128,128]{3,2,1,0:T(8,128)S(1)} async-done(((f32[32,1,128,128]{3,2,1,0:T(8,128)}), f32[32,1,128,128]{3,2,1,0:T(8,128)S(1)}, u32[]{:S(2)}, u32[]{:S(2)}) %all-to-all-start.4) | async-done | bytes 2097184 | tf_op jit(solution)/shard_map/all_to_all | solution.py:59
  176.8 6.2 all-to-all-start.1
  188.3 4.4 all-to-all-start.5
  192.9 26.2 %all-to-all-done.5 = f32[32,1,128,128]{3,0,1,2:T(8,128)S(1)} async-done(((f32[32,1,128,128]{3,0,1,2:T(8,128)}), f32[32,1,128,128]{3,0,1,2:T(8,128)S(1)}, u32[]{:S(2)}, u32[]{:S(2)}) %all-to-all-start.5) | async-done | bytes 2097184 | tf_op jit(solution)/shard_map/all_to_all | solution.py:58
  221.6 20.6 %scatter_fusion.1 = f32[17,16,128]{2,1,0:T(8,128)S(1)} fusion(f32[17,16,128]{2,1,0:T(8,128)S(1)} %broadcast.31.clone, s32[256]{0:T(256)S(1)} %reshape.132, f32[256,16,128]{2,1,0:T(8,128)} %bitcast.88), kind=kCustom, calls=%fused_computation.2 | custom fusion | flops 524288 | bytes 6292480 | tf_op jit(solution)/shard_map/scatter-add | solution.py:73
  242.9 74.1 %psum.43 = f32[]{:T(128)} all-reduce(f32[]{:T(128)} %multiply_reduce_fusion.4), channel_id=1, replica_groups=mesh['cells'=32,'modes'=8] {'cells','modes'}, use_global_device_ids=true, to_apply=%region_7.0 | all-reduce | flops 1 | bytes 8 | tf_op jit(solution)/shard_map/psum | solution.py:131
  318.3 72.6 %psum.44 = f32[]{:T(128)} all-reduce(f32[]{:T(128)} %get-tuple-element.4), channel_id=1, replica_groups=mesh['cells'=32,'modes'=8] {'cells','modes'}, use_global_device_ids=true, to_apply=%region_9.0 | all-reduce | flops 1 | bytes 8 | tf_op jit(solution)/shard_map/psum | solution.py:134
  391.6 9.3 %all_to_all.118 = f32[16,8,256]{2,0,1:T(8,128)S(1)} all-to-all(f32[16,8,256]{2,0,1:T(8,128)S(1)} %bitcast.100), channel_id=1, replica_groups=mesh['cells'=32,'modes'=8] {'modes'}, dimensions={1} | all-to-all | bytes 262144 | tf_op jit(solution)/shard_map/all_to_all | solution.py:20
  404.2 5.6 scatter_fusion.2
  409.8 6.3 all-to-all-start.8
  418.4 46.4 %all-to-all-done.8 = f32[32,1,128,128]{3,2,1,0:T(8,128)S(1)} async-done(((f32[32,1,128,128]{3,2,1,0:T(8,128)}), f32[32,1,128,128]{3,2,1,0:T(8,128)S(1)}, u32[]{:S(2)}, u32[]{:S(2)}) %all-to-all-start.8) | async-done | bytes 2097184 | tf_op jit(solution)/shard_map/all_to_all | solution.py:59
  464.8 5.6 all-to-all-start.7
  476.3 4.4 all-to-all-start.9
  483.6 23.4 %all-to-all-done.9 = f32[32,1,128,128]{3,0,1,2:T(8,128)S(1)} async-done(((f32[32,1,128,128]{3,0,1,2:T(8,128)}), f32[32,1,128,128]{3,0,1,2:T(8,128)S(1)}, u32[]{:S(2)}, u32[]{:S(2)}) %all-to-all-start.9) | async-done | bytes 2097184 | tf_op jit(solution)/shard_map/all_to_all | solution.py:58
  509.6 20.6 %scatter_fusion.3 = f32[17,16,128]{2,1,0:T(8,128)S(1)} fusion(f32[17,16,128]{2,1,0:T(8,128)S(1)} %broadcast.31, s32[256]{0:T(256)S(1)} %reshape.132, f32[256,16,128]{2,1,0:T(8,128)} %bitcast.87), kind=kCustom, calls=%fused_computation.4 | custom fusion | flops 524288 | bytes 6292480 | tf_op jit(solution)/shard_map/scatter-add | solution.py:73
  530.8 74.1 %psum.45 = f32[]{:T(128)} all-reduce(f32[]{:T(128)} %multiply_reduce_fusion.2), channel_id=1, replica_groups=mesh['cells'=32,'modes'=8] {'cells','modes'}, use_global_device_ids=true, to_apply=%region_13.0 | all-reduce | flops 1 | bytes 8 | tf_op jit(solution)/shard_map/psum | solution.py:131
  607.5 73.0 %psum.46 = f32[]{:T(128)} all-reduce(f32[]{:T(128)} %get-tuple-element.2), channel_id=1, replica_groups=mesh['cells'=32,'modes'=8] {'cells','modes'}, use_global_device_ids=true, to_apply=%region_15.0 | all-reduce | flops 1 | bytes 8 | tf_op jit(solution)/shard_map/psum | solution.py:131
  683.2 73.9 %psum.47 = f32[]{:T(128)} all-reduce(f32[]{:T(128)} %multiply_reduce_fusion), channel_id=1, replica_groups=mesh['cells'=32,'modes'=8] {'cells','modes'}, use_global_device_ids=true, to_apply=%region_17.0 | all-reduce | flops 1 | bytes 8 | tf_op jit(solution)/shard_map/psum | solution.py:134
  (60 shorter events, 47.9 us)
Async XLA Ops:
  0.6 111.5 %copy-start = (f32[9,128,128]{2,1,0:T(8,128)S(1)}, f32[9,128,128]{2,1,0:T(8,128)}, u32[]{:S(2)}) copy-start(f32[9,128,128]{2,1,0:T(8,128)} %param.7) | copy-start | bytes 1769476
  0.6 112.7 %copy-start.2 = (bf16[2,9,128,128]{3,2,1,0:T(8,128)(2,1)S(1)}, bf16[2,9,128,128]{3,2,1,0:T(8,128)(2,1)}, u32[]{:S(2)}) copy-start(bf16[2,9,128,128]{3,2,1,0:T(8,128)(2,1)} %param.9) | copy-start | bytes 1769476
  7.3 91.5 %all-to-all-start.2 = ((s32[32,1,8]{2,1,0:T(1,128)}), s32[32,1,8]{2,1,0:T(1,128)S(1)}, u32[]{:S(2)}, u32[]{:S(2)}) async-start(s32[32,1,8]{2,1,0:T(1,128)} %broadcast_in_dim.2), calls=%async_computation.2 | async-start | bytes 32768 | tf_op jit(solution)/shard_map/all_to_all | solution.py:66
  98.8 9.2 %all-to-all-start = ((f32[16,8,256]{2,0,1:T(8,128)}), f32[16,8,256]{2,0,1:T(8,128)S(1)}, u32[]{:S(2)}, u32[]{:S(2)}) async-start(f32[16,8,256]{2,0,1:T(8,128)} %bitcast.86), calls=%async_computation | async-start | bytes 262144 | tf_op jit(solution)/shard_map/all_to_all | solution.py:20
  108.0 12.9 %all-to-all-start.3 = ((s32[32,1,8]{0,1,2:T(1,128)}), s32[32,1,8]{0,1,2:T(1,128)S(1)}, u32[]{:S(2)}, u32[]{:S(2)}) async-start(s32[32,1,8]{0,1,2:T(1,128)} %copy.64), calls=%async_computation.3 | async-start | bytes 8192 | tf_op jit(solution)/shard_map/all_to_all | solution.py:65
  120.9 56.0 %all-to-all-start.4 = ((f32[32,1,128,128]{3,2,1,0:T(8,128)}), f32[32,1,128,128]{3,2,1,0:T(8,128)S(1)}, u32[]{:S(2)}, u32[]{:S(2)}) async-start(f32[32,1,128,128]{3,2,1,0:T(8,128)} %bitcast.11), calls=%async_computation.4 | async-start | bytes 4194304 | tf_op jit(solution)/shard_map/all_to_all | solution.py:59
  176.8 11.5 %all-to-all-start.1 = ((f32[8,16,256]{2,1,0:T(8,128)}), f32[8,16,256]{2,1,0:T(8,128)S(1)}, u32[]{:S(2)}, u32[]{:S(2)}) async-start(f32[8,16,256]{2,1,0:T(8,128)} %all_to_all.91), calls=%async_computation.1 | async-start | bytes 262144 | tf_op jit(solution)/shard_map/all_to_all | solution.py:78
  188.3 30.7 %all-to-all-start.5 = ((f32[32,1,128,128]{3,0,1,2:T(8,128)}), f32[32,1,128,128]{3,0,1,2:T(8,128)S(1)}, u32[]{:S(2)}, u32[]{:S(2)}) async-start(f32[32,1,128,128]{3,0,1,2:T(8,128)} %copy.67), calls=%async_computation.5 | async-start | bytes 4194304 | tf_op jit(solution)/shard_map/all_to_all | solution.py:58
  221.6 20.6 %copy-start.1 = (f32[16,2048]{1,0:T(8,128)S(1)}, f32[16,2048]{1,0:T(8,128)}, u32[]{:S(2)}) copy-start(f32[16,2048]{1,0:T(8,128)} %param.6) | copy-start | bytes 393220
  242.2 160.0 %copy-start.3 = (bf16[2,9,128,128]{3,2,1,0:T(8,128)(2,1)S(1)}, bf16[2,9,128,128]{3,2,1,0:T(8,128)(2,1)}, u32[]{:S(2)}) copy-start(bf16[2,9,128,128]{3,2,1,0:T(8,128)(2,1)} %param.9) | copy-start | bytes 1769476
  409.8 55.0 %all-to-all-start.8 = ((f32[32,1,128,128]{3,2,1,0:T(8,128)}), f32[32,1,128,128]{3,2,1,0:T(8,128)S(1)}, u32[]{:S(2)}, u32[]{:S(2)}) async-start(f32[32,1,128,128]{3,2,1,0:T(8,128)} %bitcast.23), calls=%async_computation.8 | async-start | bytes 4194304 | tf_op jit(solution)/shard_map/all_to_all | solution.py:59
  464.8 10.8 %all-to-all-start.7 = ((f32[8,16,256]{2,1,0:T(8,128)}), f32[8,16,256]{2,1,0:T(8,128)S(1)}, u32[]{:S(2)}, u32[]{:S(2)}) async-start(f32[8,16,256]{2,1,0:T(8,128)} %all_to_all.102), calls=%async_computation.7 | async-start | bytes 262144 | tf_op jit(solution)/shard_map/all_to_all | solution.py:78
  475.6 0.7 copy-start.4
  476.3 30.7 %all-to-all-start.9 = ((f32[32,1,128,128]{3,0,1,2:T(8,128)}), f32[32,1,128,128]{3,0,1,2:T(8,128)S(1)}, u32[]{:S(2)}, u32[]{:S(2)}) async-start(f32[32,1,128,128]{3,0,1,2:T(8,128)} %copy.77), calls=%async_computation.9 | async-start | bytes 4194304 | tf_op jit(solution)/shard_map/all_to_all | solution.py:58
where the time goes:
time: 762 us; the launch traced here: 759 us
  blocking collectives  454 us (60%)
  waiting for transfers between devices  153 us (20%)
  starting transfers between devices  53.7 us (7%)
  other arithmetic  51.9 us (7%)
  local copies, waits for them, and re-layouts  33.1 us (4%)
  between operations  7.86 us (1%)
    psum x3, blocking collectives, body(): product = lax.psum(jnp.sum(candidate * vector), ('cells', 'modes'))  221 us
    psum x2, blocking collectives, body(): lax.psum(jnp.sum(candidate * candidate), ('cells', 'modes'))  147 us
    all_to_all x2, waiting for transfers between devices, transposed_apply(): lax.all_to_all(outgoing, 'cells', split_axis=0, concat_axis=0, tiled=True)  93.2 us
    psum x1, blocking collectives, body(): lax.psum(jnp.sum(adjoint_source * adjoint_source), ('cells', 'modes'))  77.2 us
    all_to_all x2, waiting for transfers between devices, transposed_apply(): lax.all_to_all(lax.all_to_all(outgoing, 'cells', split_axis=0, concat_axi...  49.6 us
    scatter-add x2, other arithmetic, transposed_apply(): jax.ops.segment_sum(arrived.reshape(-1, mode_rows, block_width), arrived_...  41.2 us
  transfers between devices with their start and end apart: 9, of which 7 were waited for; matrix products, arithmetic and copies ran while one was open for 3% of the time, Pallas kernels for 0%

commit v1 on v0

v1 whole, which is shorter than its diff:
```python
import functools

import jax
import jax.numpy as jnp
from jax import lax
from jax.experimental import pallas as pl
from jax.experimental.pallas import tpu as pltpu
from jax.sharding import PartitionSpec as P

ITERS = 2
MESH = pl.DeviceIdType.MESH


def far_first(count):
    return sorted(range(count), key=lambda step: (-min(step, count - step), step))


def routing(owner_cells, target_block, cells_y, cells_z):
    entries = target_block.size
    owners = owner_cells.reshape(entries)
    targets = target_block.reshape(entries)
    here_z = lax.rem(lax.axis_index("cells"), cells_z)
    hop = lax.rem(lax.rem(owners, cells_z) - here_z + cells_z, cells_z)
    turn = sum(place * (hop == step).astype(jnp.int32) for place, step in enumerate(far_first(cells_z)))
    slot = turn * cells_y + owners // cells_z
    place = jnp.sum((slot[None, :] < slot[:, None]).astype(jnp.int32), axis=1)
    slots = cells_y * cells_z
    hit = slot[None, :] == jnp.arange(slots, dtype=jnp.int32)[:, None]
    there = jnp.any(hit, axis=1)
    where_from = jnp.where(there, jnp.sum(jnp.where(hit, place[None, :], 0), axis=1), entries)
    label = jnp.where(there, jnp.sum(jnp.where(hit, targets[None, :], 0), axis=1), -1)
    index = jnp.arange(entries, dtype=jnp.int32)
    order = jnp.sum(jnp.where(place[None, :] == index[:, None], index[None, :], 0), axis=1)
    table = jnp.concatenate([where_from, label, jnp.zeros((128 - 2 * slots,), jnp.int32)])
    return order, table.reshape(1, 128)


def kernel(
    dims,
    order_ref,
    table_ref,
    source_ref,
    coupling_ref,
    diag_ref,
    off_ref,
    solution_ref,
    next_ref,
    tables_row,
    tables_all,
    tables,
    regroup,
    raw,
    mixed,
    x_out,
    x_in_0,
    x_in_1,
    x_all,
    y_out,
    y_in,
    z_out,
    z_in,
    near_out,
    near_in,
    applied,
    sum_out,
    sum_x,
    sum_y,
    sum_z,
    table_sems,
    local_sem,
    regroup_sems,
    x_sems,
    y_sems,
    z_sems,
    near_sems,
    sum_x_sems,
    sum_y_sems,
    sum_z_sems,
):
    ny, nz, nm, terms, blocks_here = dims
    modes_total, block = coupling_ref.shape[1], off_ref.shape[-1]
    rows = modes_total // nm
    entries = terms * blocks_here
    slab = nm * blocks_here
    width = blocks_here * block
    turns = far_first(nz)
    cuts = [min(entries, ny * step) for step in range(nz + 1)]
    chunks = [(lo, hi) for lo, hi in zip(cuts[:-1], cuts[1:]) if hi > lo]
    x_in = (x_in_0, x_in_1)

    c = lax.axis_index("cells")
    m = lax.axis_index("modes")
    y, z = lax.div(c, nz), lax.rem(c, nz)

    def x_peer(d):
        return lax.rem(m + d, nm)

    def y_peer(d):
        return lax.rem(y + d, ny)

    def z_peer(d):
        return lax.rem(z + d, nz)

    def x_id(d):
        return (c, x_peer(d))

    def y_id(d):
        return (y_peer(d) * nz + z, m)

    def z_id(d):
        return (y * nz + z_peer(d), m)

    everyone = (
        [x_id(d) for d in range(1, nm)] + [y_id(d) for d in range(1, ny)] + [z_id(d) for d in range(1, nz)]
    )
    barrier = pltpu.get_barrier_semaphore()
    for device in everyone:
        pl.semaphore_signal(barrier, inc=1, device_id=device, device_id_type=MESH)

    started = []

    def send(src, dst, sems, device):
        copy = pltpu.make_async_remote_copy(
            src_ref=src,
            dst_ref=dst,
            send_sem=sems.at[0],
            recv_sem=sems.at[1],
            device_id=device,
            device_id_type=MESH,
        )
        copy.start()
        started.append(copy)

    def arrive(dst, sems, device):
        pltpu.make_async_remote_copy(
            src_ref=dst,
            dst_ref=dst,
            send_sem=sems.at[0],
            recv_sem=sems.at[1],
            device_id=device,
            device_id_type=MESH,
        ).wait_recv()

    def sum_start(at, tile):
        sum_out[at, 0] = tile
        sum_x[at, m] = tile
        for d in range(1, nm):
            send(sum_out.at[at, 0], sum_x.at[at, m], sum_x_sems.at[at, d], x_id(d))

    def sum_second(at):
        for d in range(1, nm):
            arrive(sum_x.at[at, x_peer(nm - d)], sum_x_sems.at[at, d], x_id(d))
        tile = sum_x[at, 0]
        for i in range(1, nm):
            tile = tile + sum_x[at, i]
        sum_out[at, 1] = tile
        sum_y[at, y] = tile
        for d in range(1, ny):
            send(sum_out.at[at, 1], sum_y.at[at, y], sum_y_sems.at[at, d], y_id(d))

    def sum_third(at):
        for d in range(1, ny):
            arrive(sum_y.at[at, y_peer(ny - d)], sum_y_sems.at[at, d], y_id(d))
        tile = sum_y[at, 0]
        for i in range(1, ny):
            tile = tile + sum_y[at, i]
        sum_out[at, 2] = tile
        sum_z[at, z] = tile
        for d in range(1, nz):
            send(sum_out.at[at, 2], sum_z.at[at, z], sum_z_sems.at[at, d], z_id(d))

    def sum_end(at):
        for d in range(1, nz):
            arrive(sum_z.at[at, z_peer(nz - d)], sum_z_sems.at[at, d], z_id(d))
        tile = sum_z[at, 0]
        for i in range(1, nz):
            tile = tile + sum_z[at, i]
        return jnp.sum(tile, axis=1, keepdims=True)

    def pack(lanes):
        line = lax.broadcasted_iota(jnp.int32, (8, 128), 0)
        tile = jnp.zeros((8, 128), jnp.float32)
        for i, value in enumerate(lanes):
            tile = jnp.where(line == i, jnp.broadcast_to(value, (8, 128)), tile)
        return tile

    def cell_block(ref, t):
        return ref[:, t * block : (t + 1) * block]

    def lanes_of(product):
        total = product(0)
        for t in range(1, slab):
            total = total + product(t)
        return jnp.sum(total, axis=0, keepdims=True)

    def regroup_start(at, src):
        for d in range(1, nm):
            columns = pl.ds(pl.multiple_of(x_peer(d) * width, width), width)
            send(src.at[:, columns], regroup.at[at, m], regroup_sems.at[at, d], x_id(d))
        own = pl.ds(pl.multiple_of(m * width, width), width)
        regroup[at, m] = src[:, own]

    def regroup_end(at):
        for d in range(1, nm):
            arrive(regroup.at[at, x_peer(nm - d)], regroup_sems.at[at, d], x_id(d))

    def mix(at, k):
        vector = regroup[at].reshape(modes_total, width)
        raw[at, k] = lax.dot_general(
            coupling_ref[k],
            vector,
            (((0,), (0,)), ((), ())),
            precision=lax.Precision.HIGHEST,
            preferred_element_type=jnp.float32,
        )

    def mix_and_sum(at):
        third = (terms + 2) // 3
        for k in range(0, third):
            mix(at, k)
        sum_second(at)
        for k in range(third, min(terms, 2 * third)):
            mix(at, k)
        sum_third(at)
        for k in range(min(terms, 2 * third), terms):
            mix(at, k)
        return sum_end(at)

    def far_and_near(at):
        landing = x_in[at]
        x_all[at, :, entries] = jnp.zeros((nm, rows, block), jnp.float32)
        for j, (lo, hi) in enumerate(chunks):
            for place in range(lo, hi):
                entry = order_ref[place]
                product = jnp.dot(mixed[entry], off_ref[entry], preferred_element_type=jnp.float32)
                x_out[at, place] = product.reshape(nm, rows, block)
            for d in range(1, nm):
                send(
                    x_out.at[at, lo:hi, x_peer(d)],
                    landing.at[m, lo:hi],
                    x_sems.at[at, j, d],
                    x_id(d),
                )
            x_all[at, m, lo:hi] = x_out[at, lo:hi, m]
        for b in range(blocks_here):
            total = jnp.dot(mixed[b * terms], diag_ref[b * terms], preferred_element_type=jnp.float32)
            for k in range(1, terms):
                total = total + jnp.dot(
                    mixed[b * terms + k], diag_ref[b * terms + k], preferred_element_type=jnp.float32
                )
            near_out[at, :, :, b * block : (b + 1) * block] = total.reshape(nm, rows, block)
        for d in range(1, nm):
            send(near_out.at[at, x_peer(d)], near_in.at[at, m], near_sems.at[at, d], x_id(d))
        near_in[at, m] = near_out[at, m]

        def hand_on(i):
            if i < len(chunks):
                lo, hi = chunks[i]
                for d in range(1, nm):
                    giver = x_peer(nm - d)
                    arrive(landing.at[giver, lo:hi], x_sems.at[at, i, d], x_id(d))
                    x_all[at, giver, lo:hi] = landing[giver, lo:hi]
            for d in range(ny):
                slot = i * ny + y_peer(d)
                for giver in range(nm):
                    tile = x_all[at, giver, tables[y, giver, 0, slot]]
                    if d:
                        y_out[at, i, d, giver] = tile
                    else:
                        y_in[at, i, y, giver] = tile
                if d:
                    send(y_out.at[at, i, d], y_in.at[at, i, y], y_sems.at[at, i, d], y_id(d))

        def gather(i):
            for d in range(1, ny):
                arrive(y_in.at[at, i, y_peer(ny - d)], y_sems.at[at, i, d], y_id(d))
            slot = ny * nz + i * ny + y

            def add(step, totals):
                giver_y, giver = lax.div(step, nm), lax.rem(step, nm)
                label = tables[giver_y, giver, 0, slot]
                tile = y_in[at, i, giver_y, giver]
                return tuple(total + jnp.where(label == t, tile, 0.0) for t, total in enumerate(totals))

            zero = jnp.zeros((rows, block), jnp.float32)
            totals = lax.fori_loop(0, ny * nm, add, (zero,) * slab)
            d = turns[i]
            for t in range(slab):
                if d:
                    z_out[at, i, t] = totals[t]
                else:
                    z_in[at, z, t] = totals[t]
            if d:
                send(z_out.at[at, i], z_in.at[at, z], z_sems.at[at, d], z_id(d))

        lag = 1
        for i in range(nz + lag):
            if i < nz:
                hand_on(i)
            if i >= lag:
                gather(i - lag)
        for d in range(1, nm):
            arrive(near_in.at[at, x_peer(nm - d)], near_sems.at[at, d], x_id(d))
        for d in range(1, nz):
            arrive(z_in.at[at, z_peer(nz - d)], z_sems.at[at, d], z_id(d))
        for t in range(slab):
            b = t % blocks_here
            total = near_in[at, t // blocks_here, :, b * block : (b + 1) * block]
            for giver in range(nz):
                total = total + z_in[at, giver, t]
            applied[at, :, t * block : (t + 1) * block] = total

    def round_mixed(value):
        for k in range(terms):
            rounded = value(k).astype(jnp.bfloat16)
            for b in range(blocks_here):
                mixed[b * terms + k] = rounded[:, b * block : (b + 1) * block]

    first, second = applied.at[0], applied.at[1]

    pl.semaphore_wait(barrier, len(everyone))
    regroup_start(0, source_ref)
    tables_row[m] = table_ref[...]
    for d in range(1, nm):
        send(table_ref, tables_row.at[m], table_sems.at[0, d], x_id(d))
    sum_start(0, pack([lanes_of(lambda t: cell_block(source_ref, t) * cell_block(source_ref, t))]))
    for d in range(1, nm):
        arrive(tables_row.at[x_peer(nm - d)], table_sems.at[0, d], x_id(d))
    tables_all[y] = tables_row[...]
    for d in range(1, ny):
        send(tables_row, tables_all.at[y], table_sems.at[1, d], y_id(d))
    regroup_end(0)
    sums = mix_and_sum(0)
    for d in range(1, ny):
        arrive(tables_all.at[y_peer(ny - d)], table_sems.at[1, d], y_id(d))
    tables_copy = pltpu.make_async_copy(tables_all, tables, local_sem)
    tables_copy.start()
    size = jnp.sqrt(sums[0:1])
    shrink = 1.0 / size
    round_mixed(lambda k: raw[0, k] * shrink)
    tables_copy.wait()
    far_and_near(0)

    regroup_start(1, first)
    sum_start(
        1,
        pack(
            [
                lanes_of(lambda t: cell_block(first, t) * cell_block(source_ref, t)),
                lanes_of(lambda t: cell_block(first, t) * cell_block(first, t)),
            ]
        ),
    )
    regroup_end(1)
    sums = mix_and_sum(1)
    h00 = sums[0:1] * shrink
    h10 = jnp.sqrt(jnp.maximum(sums[1:2] - h00 * h00, 0.0))
    lean = h00 * shrink
    shrink_1 = 1.0 / h10
    round_mixed(lambda k: (raw[1, k] - lean * raw[0, k]) * shrink_1)
    far_and_near(1)

    def basis_0(t):
        return cell_block(source_ref, t) * shrink

    def basis_1(t):
        return (cell_block(first, t) - lean * cell_block(source_ref, t)) * shrink_1

    sum_start(
        2,
        pack(
            [
                lanes_of(lambda t: cell_block(second, t) * basis_0(t)),
                lanes_of(lambda t: cell_block(second, t) * basis_1(t)),
                lanes_of(lambda t: cell_block(second, t) * cell_block(second, t)),
                lanes_of(lambda t: basis_0(t) * basis_1(t)),
                lanes_of(lambda t: basis_1(t) * basis_1(t)),
            ]
        ),
    )
    sum_second(2)
    sum_third(2)
    sums = sum_end(2)
    h01, cross = sums[0:1], sums[3:4]
    h11 = sums[1:2] - h01 * cross
    h21 = jnp.sqrt(
        jnp.maximum(
            sums[2:3]
            - 2.0 * h01 * h01
            - 2.0 * h11 * sums[1:2]
            + h01 * h01
            + h11 * h11 * sums[4:5]
            + 2.0 * h01 * h11 * cross,
            0.0,
        )
    )

    r00 = jnp.sqrt(h00 * h00 + h10 * h10)
    cos0, sin0 = h00 / r00, h10 / r00
    g1 = -sin0 * size
    g0 = cos0 * size
    r01 = cos0 * h01 + sin0 * h11
    low = cos0 * h11 - sin0 * h01
    r11 = jnp.sqrt(low * low + h21 * h21)
    g1 = (low / r11) * g1
    y1 = g1 / r11
    y0 = (g0 - r01 * y1) / r00
    grow = size / h21
    for t in range(slab):
        v0, v1 = basis_0(t), basis_1(t)
        solution_ref[:, t * block : (t + 1) * block] = y0 * v0 + y1 * v1
        next_ref[:, t * block : (t + 1) * block] = (cell_block(second, t) - h01 * v0 - h11 * v1) * grow

    for copy in started:
        copy.wait_send()


def body(cells_y, cells_z, adjoint_source, coupling, diag_blocks, off_blocks, owner_cells, target_block):
    nm = lax.axis_size("modes")
    blocks_here, terms, block = diag_blocks.shape[:3]
    modes_total = coupling.shape[1]
    entries = terms * blocks_here
    rows = modes_total // nm
    slab = nm * blocks_here
    width = blocks_here * block
    order, table = routing(owner_cells, target_block, cells_y, cells_z)
    dims = (cells_y, cells_z, nm, terms, blocks_here)
    f32 = jnp.float32
    chunk_count = -(-entries // cells_y)
    dma = pltpu.SemaphoreType.DMA
    vmem = pl.BlockSpec(memory_space=pltpu.VMEM)
    return pl.pallas_call(
        functools.partial(kernel, dims),
        out_shape=[jax.ShapeDtypeStruct(adjoint_source.shape, f32)] * 2,
        in_specs=[pl.BlockSpec(memory_space=pltpu.SMEM)] + [vmem] * 5,
        out_specs=[vmem, vmem],
        scratch_shapes=[
            pltpu.VMEM((nm, 1, 128), jnp.int32),
            pltpu.VMEM((cells_y, nm, 1, 128), jnp.int32),
            pltpu.SMEM((cells_y, nm, 1, 128), jnp.int32),
            pltpu.VMEM((2, nm, rows, width), f32),
            pltpu.VMEM((2, terms, modes_total, width), f32),
            pltpu.VMEM((entries, modes_total, block), jnp.bfloat16),
            pltpu.VMEM((2, entries, nm, rows, block), f32),
            pltpu.VMEM((nm, entries, rows, block), f32),
            pltpu.VMEM((nm, entries, rows, block), f32),
            pltpu.VMEM((2, nm, entries + 1, rows, block), f32),
            pltpu.VMEM((2, cells_z, cells_y, nm, rows, block), f32),
            pltpu.VMEM((2, cells_z, cells_y, nm, rows, block), f32),
            pltpu.VMEM((2, cells_z, slab, rows, block), f32),
            pltpu.VMEM((2, cells_z, slab, rows, block), f32),
            pltpu.VMEM((2, nm, rows, width), f32),
            pltpu.VMEM((2, nm, rows, width), f32),
            pltpu.VMEM((2, rows, slab * block), f32),
            pltpu.VMEM((3, 3, 8, 128), f32),
            pltpu.VMEM((3, nm, 8, 128), f32),
            pltpu.VMEM((3, cells_y, 8, 128), f32),
            pltpu.VMEM((3, cells_z, 8, 128), f32),
            dma((2, max(nm, cells_y), 2)),
            dma,
            dma((2, nm, 2)),
            dma((2, chunk_count, nm, 2)),
            dma((2, cells_z, cells_y, 2)),
            dma((2, cells_z, 2)),
            dma((2, nm, 2)),
            dma((3, nm, 2)),
            dma((3, cells_y, 2)),
            dma((3, cells_z, 2)),
        ],
        compiler_params=pltpu.CompilerParams(
            collective_id=0, has_side_effects=True, vmem_limit_bytes=48 * 1024 * 1024
        ),
    )(
        order,
        table,
        adjoint_source,
        coupling,
        diag_blocks.reshape(entries, block, block),
        off_blocks.reshape(entries, block, block),
    )


def solution(mesh, cells_z=8):
    cells_y = mesh.shape["cells"] // cells_z
    placed = (
        P("modes", "cells"),
        P(),
        P(("cells", "modes"), None, None, None),
        P(("cells", "modes"), None, None, None),
        P(("cells", "modes"), None, None),
        P(("cells", "modes"), None),
    )
    return jax.shard_map(
        functools.partial(body, cells_y, cells_z),
        mesh=mesh,
        in_specs=placed,
        out_specs=(P("modes", "cells"), P("modes", "cells")),
        check_vma=False,
    )
```

time: 762 us -> 139 us (0.18)
  blocking collectives: 454 us -> 0 us
  waiting for transfers between devices: 153 us -> 0 us
  Pallas kernels: 0 us -> 130 us
  starting transfers between devices: 53.7 us -> 0 us
  other arithmetic: 51.9 us -> 1.25 us
  local copies, waits for them, and re-layouts: 33.1 us -> 6.84 us
    psum x6 -> x0, blocking collectives: 445 us -> none  [the longest x3 221 us: body(): product = lax.psum(jnp.sum(candidate * vector), ('cells', 'modes'))]
    all_to_all x9 -> x0, waiting for transfers between devices: 153 us -> none  [the longest x2 93.2 us: transposed_apply(): lax.all_to_all(outgoing, 'cells', split_axis=0, concat_axis=0, tiled=True)]
    pallas_call x0 -> x1, Pallas kernels: none -> 130 us  [body(): pl.pallas_call(functools.partial(kernel, dims), out_shape=[jax.ShapeDtype...]
    all_to_all x9 -> x0, starting transfers between devices: 53.7 us -> none  [the longest x2 13.1 us: transposed_apply(): lax.all_to_all(outgoing, 'cells', split_axis=0, concat_axis=0, tiled=True)]
    scatter-add x2 -> x0, other arithmetic: 41.2 us -> none  [transposed_apply(): jax.ops.segment_sum(arrived.reshape(-1, mode_rows, block_width), arrived_...]
    all_to_all x12 -> x0, local copies, waits for them, and re-layouts: 14.1 us -> none  [the longest x2 5.14 us: transposed_apply(): lax.all_to_all(lax.all_to_all(outgoing, 'cells', split_axis=0, concat_axi...]
    scatter x3 -> x0, local copies, waits for them, and re-layouts: 11.8 us -> none  [the longest x2 11.2 us: transposed_apply(): outgoing = jnp.zeros((cell_groups * slot_count, modes_total, block_width)...]
    all_to_all x1 -> x0, blocking collectives: 9.34 us -> none  [transposed_apply(): lax.all_to_all(vector_in, 'modes', split_axis=1, concat_axis=0, tiled=True)]
  transfers between devices with their start and end apart: 9 -> 0, of which waited for: 7 -> 0; matrix products, arithmetic and copies ran while one was open for 3% -> 0% of each run, Pallas kernels for 0% -> 0%
where the time goes in v1:
time: 139 us
  Pallas kernels  130 us (94%)
  local copies, waits for them, and re-layouts  6.84 us (5%)
    pallas_call x1, Pallas kernels, body(): pl.pallas_call(functools.partial(kernel, dims), out_shape=[jax.ShapeDtype...  130 us
    unnamed x15, local copies, waits for them, and re-layouts  6.67 us

profile of v1, /device:TPU:1, one launch (start us, length us, event | category | flops | bytes accessed | tf_op | source)
XLA Modules:
  0.0 138.8 jit_solution(8667680292407989850)
XLA Ops:
  0.6 0.0 copy-start.4
  0.6 0.5 broadcast.309
  1.2 0.2 copy-done.4
  1.3 0.7 reduce.3
  2.0 0.1 reshape.134
  2.1 0.2 convert_reduce_fusion
  2.3 0.1 select_reduce_fusion.2.order_ref
  2.4 0.0 copy-start.5
  2.4 0.1 fusion
  2.5 0.6 copy-done.5
  3.1 0.1 broadcast_in_dim.55
  3.2 0.1 select_reduce_fusion.1
  3.3 0.1 add_bitcast_fusion.table_ref
  3.4 0.0 copy-start
  3.4 1.1 copy-done
  4.4 0.0 copy-start.1
  4.4 1.1 copy-done.1
  5.5 0.0 copy-start.2
  5.5 1.1 copy-done.2
  6.6 0.0 copy-start.3
  6.6 0.9 copy-done.3
  7.5 130.0 %shard_map.77 = (f32[16,2048]{1,0:T(8,128)S(1)}, f32[16,2048]{1,0:T(8,128)S(1)}) custom-call(s32[18]{0:T(128)S(1)} %select_reduce_fusion.2.order_ref, s32[1,128]{1,0:T(1,128)S(1)} %add_bitcast_fusion.table_ref, f32[16,2048]{1,0:T(8,128)S(1)} %copy-done.3, f32[9,128,128]{2,1,0:T(8,128)S(1)} %copy-done, bf16[18,128,128]{2,1,0:T(8,128)(2,1)S(1)} %bitcast.5, ...), custom_call_target="tpu_custom_call" | custom-call | tf_op jit(solution)/shard_map/pallas_call | solution.py:432
  137.5 0.7 copy.10
  138.1 0.7 copy.11
  (3 shorter events, 0.0 us)
Async XLA Ops:
  0.6 0.7 copy-start.4
  2.4 0.7 copy-start.5
  3.4 1.1 copy-start
  4.4 1.1 copy-start.1
  5.5 1.1 copy-start.2
  6.6 0.9 copy-start.3

commit v2 on v1

v2 whole, which is shorter than its diff:
```python
import functools

import jax
import jax.numpy as jnp
from jax import lax
from jax.experimental import pallas as pl
from jax.experimental.pallas import tpu as pltpu
from jax.sharding import PartitionSpec as P

MESH = pl.DeviceIdType.MESH


def far_first(count):
    return sorted(range(count), key=lambda step: (-min(step, count - step), step))


def kernel(
    dims,
    owner_ref,
    target_ref,
    source_hbm,
    coupling_hbm,
    diag_hbm,
    off_hbm,
    solution_ref,
    next_ref,
    source_ref,
    coupling_ref,
    diag_ref,
    off_ref,
    load_sems,
    order_ref,
    table_out,
    tables_row,
    tables_all,
    sources,
    tables,
    regroup,
    mixers,
    mixed,
    x_out,
    x_in_0,
    x_in_1,
    x_all,
    y_out,
    y_in,
    z_out,
    z_in,
    near_out,
    near_in,
    far_sum,
    applied,
    sum_out,
    sum_x,
    sum_y,
    sum_z,
    table_sems,
    local_sems,
    regroup_sems,
    x_sems,
    y_sems,
    z_sems,
    near_sems,
    sum_x_sems,
    sum_y_sems,
    sum_z_sems,
):
    ny, nz, nm, terms, blocks_here = dims
    modes_total, block = coupling_ref.shape[1], off_ref.shape[-1]
    rows = modes_total // nm
    entries = terms * blocks_here
    slab = nm * blocks_here
    width = blocks_here * block
    turns = far_first(nz)
    turn_of = {d: i for i, d in enumerate(turns)}
    cuts = [min(entries, ny * step) for step in range(nz + 1)]
    chunks = [(lo, hi) for lo, hi in zip(cuts[:-1], cuts[1:]) if hi > lo]
    x_in = (x_in_0, x_in_1)

    c = lax.axis_index("cells")
    m = lax.axis_index("modes")
    y, z = lax.div(c, nz), lax.rem(c, nz)

    def x_peer(d):
        return lax.rem(m + d, nm)

    def y_peer(d):
        return lax.rem(y + d, ny)

    def z_peer(d):
        return lax.rem(z + d, nz)

    def x_id(d):
        return (c, x_peer(d))

    def y_id(d):
        return (y_peer(d) * nz + z, m)

    def z_id(d):
        return (y * nz + z_peer(d), m)

    everyone = (
        [x_id(d) for d in range(1, nm)]
        + [y_id(d) for d in range(1, ny)]
        + [z_id(d) for d in sorted({1, nz - 1})]
    )
    barrier = pltpu.get_barrier_semaphore()
    for device in everyone:
        pl.semaphore_signal(barrier, inc=1, device_id=device, device_id_type=MESH)
    loads = [
        pltpu.make_async_copy(src, dst, load_sems.at[i])
        for i, (src, dst) in enumerate(
            [
                (source_hbm, source_ref),
                (coupling_hbm, coupling_ref),
                (off_hbm, off_ref),
                (diag_hbm, diag_ref),
            ]
        )
    ]
    for load in loads:
        load.start()

    started = []

    def send(src, dst, sems, device):
        copy = pltpu.make_async_remote_copy(
            src_ref=src,
            dst_ref=dst,
            send_sem=sems.at[0],
            recv_sem=sems.at[1],
            device_id=device,
            device_id_type=MESH,
        )
        copy.start()
        started.append(copy)

    def arrive(dst, sems, device):
        pltpu.make_async_remote_copy(
            src_ref=dst,
            dst_ref=dst,
            send_sem=sems.at[0],
            recv_sem=sems.at[1],
            device_id=device,
            device_id_type=MESH,
        ).wait_recv()

    def sum_all(tile):
        stages = (
            (sum_x, sum_x_sems, m, nm, x_peer, x_id),
            (sum_y, sum_y_sems, y, ny, y_peer, y_id),
            (sum_z, sum_z_sems, z, nz, z_peer, z_id),
        )
        for at, (held, sems, here, count, peer, device) in enumerate(stages):
            sum_out[at] = tile
            for d in range(1, count):
                send(sum_out.at[at], held.at[here], sems.at[d], device(d))
            held[here] = tile
            for d in range(1, count):
                arrive(held.at[peer(count - d)], sems.at[d], device(d))
            tile = held[0]
            for i in range(1, count):
                tile = tile + held[i]
        return jnp.sum(tile, axis=1, keepdims=True)

    def pack(lanes):
        line = lax.broadcasted_iota(jnp.int32, (8, 128), 0)
        tile = jnp.zeros((8, 128), jnp.float32)
        for i, value in enumerate(lanes):
            tile = jnp.where(line == i, jnp.broadcast_to(value, (8, 128)), tile)
        return tile

    def cell_block(ref, t):
        return ref[:, t * block : (t + 1) * block]

    def dot_lanes(left, right):
        total = cell_block(left, 0) * cell_block(right, 0)
        for t in range(1, slab):
            total = total + cell_block(left, t) * cell_block(right, t)
        return jnp.sum(total, axis=0, keepdims=True)

    def regroup_start(at, src):
        for d in range(1, nm):
            columns = pl.ds(pl.multiple_of(x_peer(d) * width, width), width)
            send(src.at[:, columns], regroup.at[at, m], regroup_sems.at[at, d], x_id(d))
        own = pl.ds(pl.multiple_of(m * width, width), width)
        regroup[at, m] = src[:, own]

    def regroup_end(at):
        for d in range(1, nm):
            arrive(regroup.at[at, x_peer(nm - d)], regroup_sems.at[at, d], x_id(d))
        return regroup[at].reshape(modes_total, width)

    def split(value):
        high = value.astype(jnp.bfloat16)
        return high, (value - high.astype(jnp.float32)).astype(jnp.bfloat16)

    def mix(vector):
        high, low = split(vector)
        stacked = jnp.concatenate([high, high, low], axis=0)
        for k in range(terms):
            value = jnp.dot(mixers[k], stacked, preferred_element_type=jnp.float32)
            high_k, low_k = split(value)
            for b in range(blocks_here):
                mixed[b * terms + k, 0] = high_k[:, b * block : (b + 1) * block]
                mixed[b * terms + k, 1] = low_k[:, b * block : (b + 1) * block]

    def times(entry, blocks, at_block):
        matrix = blocks[at_block]
        return jnp.dot(mixed[entry, 0], matrix, preferred_element_type=jnp.float32) + jnp.dot(
            mixed[entry, 1], matrix, preferred_element_type=jnp.float32
        )

    def far_and_near(at, know_row=lambda: None, know_all=lambda: None):
        landing = x_in[at]
        x_all[at, :, entries] = jnp.zeros((nm, rows, block), jnp.float32)
        for j, (lo, hi) in enumerate(chunks):
            for place in range(lo, hi):
                entry = order_ref[place]
                x_out[at, place] = times(entry, off_ref, entry).reshape(nm, rows, block)
            for d in range(1, nm):
                send(
                    x_out.at[at, lo:hi, x_peer(d)],
                    landing.at[m, lo:hi],
                    x_sems.at[at, j, d],
                    x_id(d),
                )
            x_all[at, m, lo:hi] = x_out[at, lo:hi, m]

        def near():
            for b in range(blocks_here):
                total = times(b * terms, diag_ref, b * terms)
                for k in range(1, terms):
                    total = total + times(b * terms + k, diag_ref, b * terms + k)
                near_out[at, :, :, b * block : (b + 1) * block] = total.reshape(nm, rows, block)
            for d in range(1, nm):
                send(near_out.at[at, x_peer(d)], near_in.at[at, m], near_sems.at[at, d], x_id(d))
            near_in[at, m] = near_out[at, m]

        def hand_on(i):
            if i < len(chunks):
                lo, hi = chunks[i]
                for d in range(1, nm):
                    giver = x_peer(nm - d)
                    arrive(landing.at[giver, lo:hi], x_sems.at[at, i, d], x_id(d))
                    x_all[at, giver, lo:hi] = landing[giver, lo:hi]
            for d in list(range(1, ny)) + [0]:
                slot = i * ny + y_peer(d)
                for giver in range(nm):
                    tile = x_all[at, giver, sources[giver, 0, slot]]
                    if d:
                        y_out[at, i, d, giver] = tile
                    else:
                        y_in[at, i, y, giver] = tile
                if d:
                    send(y_out.at[at, i, d], y_in.at[at, i, y], y_sems.at[at, i, d], y_id(d))

        half = slab // 2
        up, down = (0, slice(0, half)), (1, slice(half, slab))

        def z_received(way, d, targets):
            came_from = d + 1 if way == 0 else (d - 1) % nz
            step = nz - 1 if way == 0 else 1
            held = z_in.at[at, way, turn_of[came_from], targets]
            arrive(held, z_sems.at[at, way, turn_of[came_from]], z_id(step))
            return held

        def gather(i):
            for d in range(1, ny):
                arrive(y_in.at[at, i, y_peer(ny - d)], y_sems.at[at, i, d], y_id(d))
            slot = ny * nz + i * ny + y

            def add(step, totals):
                giver_y, giver = lax.div(step, nm), lax.rem(step, nm)
                label = tables[giver_y, giver, 0, slot]
                tile = y_in[at, i, giver_y, giver]
                return tuple(total + jnp.where(label == t, tile, 0.0) for t, total in enumerate(totals))

            zero = jnp.zeros((rows, block), jnp.float32)
            totals = list(lax.fori_loop(0, ny * nm, add, (zero,) * slab))
            d = turns[i]
            middle = nz // 2
            everything = slice(0, slab)
            if d < middle:
                targets = up[1] if d + 1 == middle else everything
                held = z_received(0, d, targets)
                for t in range(targets.start, targets.stop):
                    totals[t] = totals[t] + held[t - targets.start]
            if d > middle or d == 0:
                targets = down[1] if (d - 1) % nz == middle else everything
                held = z_received(1, d, targets)
                for t in range(targets.start, targets.stop):
                    totals[t] = totals[t] + held[t - targets.start]
            if d == 0:
                for t in range(slab):
                    far_sum[at, :, t * block : (t + 1) * block] = totals[t]
                return
            for t in range(slab):
                z_out[at, i, t] = totals[t]
            if d <= middle:
                targets = up[1] if d == middle else everything
                send(z_out.at[at, i, targets], z_in.at[at, 0, i, targets], z_sems.at[at, 0, i], z_id(1))
            if d >= middle:
                targets = down[1] if d == middle else everything
                send(z_out.at[at, i, targets], z_in.at[at, 1, i, targets], z_sems.at[at, 1, i], z_id(nz - 1))

        know_row()
        lag = min(2, nz)
        for i in range(nz + lag):
            if i < nz:
                hand_on(i)
            if i == 1:
                near()
                know_all()
            if i >= lag:
                gather(i - lag)

    def complete(at):
        for d in range(1, nm):
            arrive(near_in.at[at, x_peer(nm - d)], near_sems.at[at, d], x_id(d))
        for t in range(slab):
            b = t % blocks_here
            applied[at, :, t * block : (t + 1) * block] = (
                near_in[at, t // blocks_here, :, b * block : (b + 1) * block] + far_sum[at, :, t * block : (t + 1) * block]
            )

    slots = ny * nz
    slot_of, target_of = [], []
    for e in range(entries):
        owner = owner_ref[e // terms, 0, e % terms]
        hop = lax.rem(lax.rem(owner, nz) - z + nz, nz)
        near_hop = jnp.minimum(hop, nz - hop)
        turn = jnp.maximum(nz - 2 * near_hop - jnp.where(2 * hop <= nz, 1, 0), 0)
        slot_of.append(turn * ny + lax.div(owner, nz))
        target_of.append(target_ref[e // terms, e % terms])
    place_of = []
    for e in range(entries):
        place = jnp.int32(0)
        for other in range(entries):
            if other != e:
                place = place + jnp.where(slot_of[other] < slot_of[e], 1, 0)
        place_of.append(place)
    for p in range(entries):
        entry = jnp.int32(0)
        for e in range(1, entries):
            entry = entry + jnp.where(place_of[e] == p, e, 0)
        order_ref[p] = jnp.minimum(entry, entries - 1)
    lane = lax.broadcasted_iota(jnp.int32, (1, 128), 1)
    there = jnp.zeros((1, 128), jnp.int32)
    before = jnp.zeros((1, 128), jnp.int32)
    label = jnp.full((1, 128), -1, jnp.int32)
    for e in range(entries):
        there = there + jnp.where(lane == slot_of[e], 1, 0)
        before = before + jnp.where(lane > slot_of[e], 1, 0)
        label = jnp.where(lane - slots == slot_of[e], target_of[e], label)
    table_out[...] = jnp.where(lane < slots, jnp.where(there > 0, before, entries), label)

    loads[0].wait()
    pl.semaphore_wait(barrier, len(everyone))
    regroup_start(0, source_ref)
    for d in range(1, nm):
        send(table_out, tables_row.at[m], table_sems.at[0, d], x_id(d))
    tables_row[m] = table_out[...]
    loads[1].wait()
    for k in range(terms):
        high, low = split(coupling_ref[k].T)
        mixers[k] = jnp.concatenate([high, low, high], axis=1)
    for d in range(1, nm):
        arrive(tables_row.at[x_peer(nm - d)], table_sems.at[0, d], x_id(d))
    for d in range(1, ny):
        send(tables_row, tables_all.at[y], table_sems.at[1, d], y_id(d))
    row_copy = pltpu.make_async_copy(tables_row, sources, local_sems.at[0])
    row_copy.start()
    tables_all[y] = tables_row[...]
    mix(regroup_end(0))
    loads[2].wait()
    loads[3].wait()

    def know_row():
        row_copy.wait()

    def know_all():
        for d in range(1, ny):
            arrive(tables_all.at[y_peer(ny - d)], table_sems.at[1, d], y_id(d))
        all_copy = pltpu.make_async_copy(tables_all, tables, local_sems.at[1])
        all_copy.start()
        all_copy.wait()

    far_and_near(0, know_row, know_all)

    regroup_start(1, far_sum.at[0])
    far = regroup_end(1)
    mix(far + near_out[0].reshape(modes_total, width))
    far_and_near(1)
    complete(0)
    complete(1)
    first, second = applied.at[0], applied.at[1]

    sums = sum_all(
        pack(
            [
                dot_lanes(source_ref, source_ref),
                dot_lanes(source_ref, first),
                dot_lanes(first, first),
                dot_lanes(source_ref, second),
                dot_lanes(first, second),
                dot_lanes(second, second),
            ]
        )
    )
    uu, uw, ww, uq, wq, qq = (sums[i : i + 1] for i in range(6))
    size = jnp.sqrt(uu)
    h00 = uw / uu
    h10 = jnp.sqrt(jnp.maximum(ww / uu - h00 * h00, 0.0))
    scale = 1.0 / h10
    h01 = (uq - h00 * uw) / uu * scale
    h11 = (wq - h00 * uq - h00 * (ww - h00 * uw)) / uu * scale * scale
    h21 = jnp.sqrt(
        jnp.maximum(
            (qq - 2.0 * h00 * wq + h00 * h00 * ww) / uu * scale * scale - h01 * h01 - h11 * h11,
            0.0,
        )
    )

    r00 = jnp.sqrt(h00 * h00 + h10 * h10)
    cos0, sin0 = h00 / r00, h10 / r00
    g1 = -sin0 * size
    g0 = cos0 * size
    r01 = cos0 * h01 + sin0 * h11
    low = cos0 * h11 - sin0 * h01
    r11 = jnp.sqrt(low * low + h21 * h21)
    y1 = (low / r11) * g1 / r11
    y0 = (g0 - r01 * y1) / r00

    sol_w = y1 * scale / size
    sol_u = y0 / size - sol_w * h00
    next_q = scale / h21
    next_w = -(h00 + h11) * next_q
    next_u = h11 * h00 * next_q - h01 / h21
    for t in range(slab):
        u, w = cell_block(source_ref, t), cell_block(first, t)
        solution_ref[:, t * block : (t + 1) * block] = sol_u * u + sol_w * w
        next_ref[:, t * block : (t + 1) * block] = next_q * cell_block(second, t) + next_w * w + next_u * u

    for copy in started:
        copy.wait_send()


def body(cells_y, cells_z, adjoint_source, coupling, diag_blocks, off_blocks, owner_cells, target_block):
    nm = lax.axis_size("modes")
    blocks_here, terms, block = diag_blocks.shape[:3]
    modes_total = coupling.shape[1]
    entries = terms * blocks_here
    rows = modes_total // nm
    slab = nm * blocks_here
    width = blocks_here * block
    dims = (cells_y, cells_z, nm, terms, blocks_here)
    f32, bf16 = jnp.float32, jnp.bfloat16
    chunk_count = -(-entries // cells_y)
    dma = pltpu.SemaphoreType.DMA
    vmem = pl.BlockSpec(memory_space=pltpu.VMEM)
    smem = pl.BlockSpec(memory_space=pltpu.SMEM)
    anywhere = pl.BlockSpec(memory_space=pl.ANY)
    return pl.pallas_call(
        functools.partial(kernel, dims),
        out_shape=[jax.ShapeDtypeStruct(adjoint_source.shape, f32)] * 2,
        in_specs=[smem, smem] + [anywhere] * 4,
        out_specs=[vmem, vmem],
        scratch_shapes=[
            pltpu.VMEM((rows, slab * block), f32),
            pltpu.VMEM((terms, modes_total, modes_total), f32),
            pltpu.VMEM((entries, block, block), bf16),
            pltpu.VMEM((entries, block, block), bf16),
            dma((4,)),
            pltpu.SMEM((entries,), jnp.int32),
            pltpu.VMEM((1, 128), jnp.int32),
            pltpu.VMEM((nm, 1, 128), jnp.int32),
            pltpu.VMEM((cells_y, nm, 1, 128), jnp.int32),
            pltpu.SMEM((nm, 1, 128), jnp.int32),
            pltpu.SMEM((cells_y, nm, 1, 128), jnp.int32),
            pltpu.VMEM((2, nm, rows, width), f32),
            pltpu.VMEM((terms, modes_total, 3 * modes_total), bf16),
            pltpu.VMEM((entries, 2, modes_total, block), bf16),
            pltpu.VMEM((2, entries, nm, rows, block), f32),
            pltpu.VMEM((nm, entries, rows, block), f32),
            pltpu.VMEM((nm, entries, rows, block), f32),
            pltpu.VMEM((2, nm, entries + 1, rows, block), f32),
            pltpu.VMEM((2, cells_z, cells_y, nm, rows, block), f32),
            pltpu.VMEM((2, cells_z, cells_y, nm, rows, block), f32),
            pltpu.VMEM((2, cells_z, slab, rows, block), f32),
            pltpu.VMEM((2, 2, cells_z, slab, rows, block), f32),
            pltpu.VMEM((2, nm, rows, width), f32),
            pltpu.VMEM((2, nm, rows, width), f32),
            pltpu.VMEM((2, rows, slab * block), f32),
            pltpu.VMEM((2, rows, slab * block), f32),
            pltpu.VMEM((3, 8, 128), f32),
            pltpu.VMEM((nm, 8, 128), f32),
            pltpu.VMEM((cells_y, 8, 128), f32),
            pltpu.VMEM((cells_z, 8, 128), f32),
            dma((2, max(nm, cells_y), 2)),
            dma((2,)),
            dma((2, nm, 2)),
            dma((2, chunk_count, nm, 2)),
            dma((2, cells_z, cells_y, 2)),
            dma((2, 2, cells_z, 2)),
            dma((2, nm, 2)),
            dma((nm, 2)),
            dma((cells_y, 2)),
            dma((cells_z, 2)),
        ],
        compiler_params=pltpu.CompilerParams(
            collective_id=0, has_side_effects=True, vmem_limit_bytes=62 * 1024 * 1024
        ),
    )(
        owner_cells.transpose(0, 2, 1),
        target_block,
        adjoint_source,
        coupling,
        diag_blocks.reshape(entries, block, block),
        off_blocks.reshape(entries, block, block),
    )


def solution(mesh, cells_z=8):
    cells_y = mesh.shape["cells"] // cells_z
    placed = (
        P("modes", "cells"),
        P(),
        P(("cells", "modes"), None, None, None),
        P(("cells", "modes"), None, None, None),
        P(("cells", "modes"), None, None),
        P(("cells", "modes"), None),
    )
    return jax.shard_map(
        functools.partial(body, cells_y, cells_z),
        mesh=mesh,
        in_specs=placed,
        out_specs=(P("modes", "cells"), P("modes", "cells")),
        check_vma=False,
    )
```

time: 139 us -> 107 us (0.77)
  Pallas kernels: 130 us -> 104 us
  local copies, waits for them, and re-layouts: 6.84 us -> 2.26 us
    pallas_call x1, Pallas kernels: 130 us -> 104 us  [body(): pl.pallas_call(functools.partial(kernel, dims), out_shape=[jax.ShapeDtype...]
    unnamed x15 -> x4, local copies, waits for them, and re-layouts: 6.67 us -> 2.26 us
where the time goes in v2:
time: 107 us
  Pallas kernels  104 us (97%)
  local copies, waits for them, and re-layouts  2.26 us (2%)
    pallas_call x1, Pallas kernels, body(): pl.pallas_call(functools.partial(kernel, dims), out_shape=[jax.ShapeDtype...  104 us
    unnamed x4, local copies, waits for them, and re-layouts  2.26 us

profile of v2, /device:TPU:1, one launch (start us, length us, event | category | flops | bytes accessed | tf_op | source)
XLA Modules:
  0.0 106.9 jit_solution(12337865978664512346)
XLA Ops:
  0.6 104.0 %shard_map.77 = (f32[16,2048]{1,0:T(8,128)}, f32[16,2048]{1,0:T(8,128)}) custom-call(s32[2,1,9]{2,1,0:T(1,128)} %bitcast.7, s32[2,9]{1,0:T(2,128)} %target_ref.1, f32[16,2048]{1,0:T(8,128)} %source_hbm.1, f32[9,128,128]{2,1,0:T(8,128)} %coupling_hbm.1, bf16[18,128,128]{2,1,0:T(8,128)(2,1)} %bitcast.5, bf16[18,128,128]{2,1,0:T(8,128)(2,1)} %bitcast.6), custom_call_target="tpu_custom_call" | custom-call | tf_op jit(solution)/shard_map/pallas_call | solution.py:464
  104.6 0.0 copy-start
  104.6 1.6 %copy.11 = f32[16,2048]{1,0:T(8,128)} copy(f32[16,2048]{1,0:T(8,128)} %get-tuple-element.4) | data formatting | bytes 262144
  106.2 0.0 copy-done
  106.2 0.7 copy.12
Async XLA Ops:
  104.6 1.6 %copy-start = (f32[16,2048]{1,0:T(8,128)S(1)}, f32[16,2048]{1,0:T(8,128)}, u32[]{:S(2)}) copy-start(f32[16,2048]{1,0:T(8,128)} %get-tuple-element.5) | copy-start | bytes 393220

commit v3 on v2

--- a/solution.py
+++ b/solution.py
@@ -36,7 +36,7 @@
     sources,
     tables,
     regroup,
-    mixers,
+    raw,
     mixed,
     x_out,
     x_in_0,
@@ -102,7 +102,7 @@
     everyone = (
         [x_id(d) for d in range(1, nm)]
         + [y_id(d) for d in range(1, ny)]
-        + [z_id(d) for d in sorted({1, nz - 1})]
+        + [z_id(d) for d in range(1, nz)]
     )
     barrier = pltpu.get_barrier_semaphore()
     for device in everyone:
@@ -145,22 +145,40 @@
             device_id_type=MESH,
         ).wait_recv()
 
-    def sum_all(tile):
-        stages = (
-            (sum_x, sum_x_sems, m, nm, x_peer, x_id),
-            (sum_y, sum_y_sems, y, ny, y_peer, y_id),
-            (sum_z, sum_z_sems, z, nz, z_peer, z_id),
-        )
-        for at, (held, sems, here, count, peer, device) in enumerate(stages):
-            sum_out[at] = tile
-            for d in range(1, count):
-                send(sum_out.at[at], held.at[here], sems.at[d], device(d))
-            held[here] = tile
-            for d in range(1, count):
-                arrive(held.at[peer(count - d)], sems.at[d], device(d))
-            tile = held[0]
-            for i in range(1, count):
-                tile = tile + held[i]
+    def sum_start(at, tile):
+        sum_out[at, 0] = tile
+        sum_x[at, m] = tile
+        for d in range(1, nm):
+            send(sum_out.at[at, 0], sum_x.at[at, m], sum_x_sems.at[at, d], x_id(d))
+
+    def sum_second(at):
+        for d in range(1, nm):
+            arrive(sum_x.at[at, x_peer(nm - d)], sum_x_sems.at[at, d], x_id(d))
+        tile = sum_x[at, 0]
+        for i in range(1, nm):
+            tile = tile + sum_x[at, i]
+        sum_out[at, 1] = tile
+        sum_y[at, y] = tile
+        for d in range(1, ny):
+            send(sum_out.at[at, 1], sum_y.at[at, y], sum_y_sems.at[at, d], y_id(d))
+
+    def sum_third(at):
+        for d in range(1, ny):
+            arrive(sum_y.at[at, y_peer(ny - d)], sum_y_sems.at[at, d], y_id(d))
+        tile = sum_y[at, 0]
+        for i in range(1, ny):
+            tile = tile + sum_y[at, i]
+        sum_out[at, 2] = tile
+        sum_z[at, z] = tile
+        for d in range(1, nz):
+            send(sum_out.at[at, 2], sum_z.at[at, z], sum_z_sems.at[at, d], z_id(d))
+
+    def sum_end(at):
+        for d in range(1, nz):
+            arrive(sum_z.at[at, z_peer(nz - d)], sum_z_sems.at[at, d], z_id(d))
+        tile = sum_z[at, 0]
+        for i in range(1, nz):
+            tile = tile + sum_z[at, i]
         return jnp.sum(tile, axis=1, keepdims=True)
 
     def pack(lanes):
@@ -173,6 +191,12 @@
     def cell_block(ref, t):
         return ref[:, t * block : (t + 1) * block]
 
+    def lanes_of(product):
+        total = product(0)
+        for t in range(1, slab):
+            total = total + product(t)
+        return jnp.sum(total, axis=0, keepdims=True)
+
     def dot_lanes(left, right):
         total = cell_block(left, 0) * cell_block(right, 0)
         for t in range(1, slab):
@@ -191,25 +215,35 @@
             arrive(regroup.at[at, x_peer(nm - d)], regroup_sems.at[at, d], x_id(d))
         return regroup[at].reshape(modes_total, width)
 
-    def split(value):
-        high = value.astype(jnp.bfloat16)
-        return high, (value - high.astype(jnp.float32)).astype(jnp.bfloat16)
-
-    def mix(vector):
-        high, low = split(vector)
-        stacked = jnp.concatenate([high, high, low], axis=0)
+    def mix_and_sum(at, vector):
+        def mix(k):
+            raw[at, k] = lax.dot_general(
+                coupling_ref[k],
+                vector,
+                (((0,), (0,)), ((), ())),
+                precision=lax.Precision.HIGHEST,
+                preferred_element_type=jnp.float32,
+            )
+
+        third = (terms + 2) // 3
+        for k in range(0, third):
+            mix(k)
+        sum_second(at)
+        for k in range(third, min(terms, 2 * third)):
+            mix(k)
+        sum_third(at)
+        for k in range(min(terms, 2 * third), terms):
+            mix(k)
+        return sum_end(at)
+
+    def round_mixed(value):
         for k in range(terms):
-            value = jnp.dot(mixers[k], stacked, preferred_element_type=jnp.float32)
-            high_k, low_k = split(value)
+            rounded = value(k).astype(jnp.bfloat16)
             for b in range(blocks_here):
-                mixed[b * terms + k, 0] = high_k[:, b * block : (b + 1) * block]
-                mixed[b * terms + k, 1] = low_k[:, b * block : (b + 1) * block]
+                mixed[b * terms + k] = rounded[:, b * block : (b + 1) * block]
 
     def times(entry, blocks, at_block):
-        matrix = blocks[at_block]
-        return jnp.dot(mixed[entry, 0], matrix, preferred_element_type=jnp.float32) + jnp.dot(
-            mixed[entry, 1], matrix, preferred_element_type=jnp.float32
-        )
+        return jnp.dot(mixed[entry], blocks[at_block], preferred_element_type=jnp.float32)
 
     def far_and_near(at, know_row=lambda: None, know_all=lambda: None):
         landing = x_in[at]
@@ -357,14 +391,12 @@
 
     loads[0].wait()
     pl.semaphore_wait(barrier, len(everyone))
+    sum_start(0, pack([dot_lanes(source_ref, source_ref)]))
     regroup_start(0, source_ref)
     for d in range(1, nm):
         send(table_out, tables_row.at[m], table_sems.at[0, d], x_id(d))
     tables_row[m] = table_out[...]
     loads[1].wait()
-    for k in range(terms):
-        high, low = split(coupling_ref[k].T)
-        mixers[k] = jnp.concatenate([high, low, high], axis=1)
     for d in range(1, nm):
         arrive(tables_row.at[x_peer(nm - d)], table_sems.at[0, d], x_id(d))
     for d in range(1, ny):
@@ -372,7 +404,10 @@
     row_copy = pltpu.make_async_copy(tables_row, sources, local_sems.at[0])
     row_copy.start()
     tables_all[y] = tables_row[...]
-    mix(regroup_end(0))
+    sums = mix_and_sum(0, regroup_end(0))
+    size = jnp.sqrt(sums[0:1])
+    shrink = 1.0 / size
+    round_mixed(lambda k: raw[0, k] * shrink)
     loads[2].wait()
     loads[3].wait()
 
@@ -388,36 +423,51 @@
 
     far_and_near(0, know_row, know_all)
 
+    first, second = applied.at[0], applied.at[1]
+    complete(0)
+    sum_start(1, pack([dot_lanes(first, source_ref), dot_lanes(first, first)]))
     regroup_start(1, far_sum.at[0])
     far = regroup_end(1)
-    mix(far + near_out[0].reshape(modes_total, width))
+    sums = mix_and_sum(1, far + near_out[0].reshape(modes_total, width))
+    h00 = sums[0:1] * shrink
+    h10 = jnp.sqrt(jnp.maximum(sums[1:2] - h00 * h00, 0.0))
+    lean = h00 * shrink
+    shrink_1 = 1.0 / h10
+    round_mixed(lambda k: (raw[1, k] - lean * raw[0, k]) * shrink_1)
     far_and_near(1)
-    complete(0)
     complete(1)
-    first, second = applied.at[0], applied.at[1]
-
-    sums = sum_all(
+
+    def basis_0(t):
+        return cell_block(source_ref, t) * shrink
+
+    def basis_1(t):
+        return (cell_block(first, t) - lean * cell_block(source_ref, t)) * shrink_1
+
+    sum_start(
+        2,
         pack(
             [
-                dot_lanes(source_ref, source_ref),
-                dot_lanes(source_ref, first),
-                dot_lanes(first, first),
-                dot_lanes(source_ref, second),
-                dot_lanes(first, second),
-                dot_lanes(second, second),
+                lanes_of(lambda t: cell_block(second, t) * basis_0(t)),
+                lanes_of(lambda t: cell_block(second, t) * basis_1(t)),
+                lanes_of(lambda t: cell_block(second, t) * cell_block(second, t)),
+                lanes_of(lambda t: basis_0(t) * basis_1(t)),
+                lanes_of(lambda t: basis_1(t) * basis_1(t)),
             ]
-        )
+        ),
     )
-    uu, uw, ww, uq, wq, qq = (sums[i : i + 1] for i in range(6))
-    size = jnp.sqrt(uu)
-    h00 = uw / uu
-    h10 = jnp.sqrt(jnp.maximum(ww / uu - h00 * h00, 0.0))
-    scale = 1.0 / h10
-    h01 = (uq - h00 * uw) / uu * scale
-    h11 = (wq - h00 * uq - h00 * (ww - h00 * uw)) / uu * scale * scale
+    sum_second(2)
+    sum_third(2)
+    sums = sum_end(2)
+    h01, cross = sums[0:1], sums[3:4]
+    h11 = sums[1:2] - h01 * cross
     h21 = jnp.sqrt(
         jnp.maximum(
-            (qq - 2.0 * h00 * wq + h00 * h00 * ww) / uu * scale * scale - h01 * h01 - h11 * h11,
+            sums[2:3]
+            - 2.0 * h01 * h01
+            - 2.0 * h11 * sums[1:2]
+            + h01 * h01
+            + h11 * h11 * sums[4:5]
+            + 2.0 * h01 * h11 * cross,
             0.0,
         )
     )
@@ -429,18 +479,14 @@
     r01 = cos0 * h01 + sin0 * h11
     low = cos0 * h11 - sin0 * h01
     r11 = jnp.sqrt(low * low + h21 * h21)
-    y1 = (low / r11) * g1 / r11
+    g1 = (low / r11) * g1
+    y1 = g1 / r11
     y0 = (g0 - r01 * y1) / r00
-
-    sol_w = y1 * scale / size
-    sol_u = y0 / size - sol_w * h00
-    next_q = scale / h21
-    next_w = -(h00 + h11) * next_q
-    next_u = h11 * h00 * next_q - h01 / h21
+    grow = size / h21
     for t in range(slab):
-        u, w = cell_block(source_ref, t), cell_block(first, t)
-        solution_ref[:, t * block : (t + 1) * block] = sol_u * u + sol_w * w
-        next_ref[:, t * block : (t + 1) * block] = next_q * cell_block(second, t) + next_w * w + next_u * u
+        v0, v1 = basis_0(t), basis_1(t)
+        solution_ref[:, t * block : (t + 1) * block] = y0 * v0 + y1 * v1
+        next_ref[:, t * block : (t + 1) * block] = (cell_block(second, t) - h01 * v0 - h11 * v1) * grow
 
     for copy in started:
         copy.wait_send()
@@ -479,8 +525,8 @@
             pltpu.SMEM((nm, 1, 128), jnp.int32),
             pltpu.SMEM((cells_y, nm, 1, 128), jnp.int32),
             pltpu.VMEM((2, nm, rows, width), f32),
-            pltpu.VMEM((terms, modes_total, 3 * modes_total), bf16),
-            pltpu.VMEM((entries, 2, modes_total, block), bf16),
+            pltpu.VMEM((2, terms, modes_total, width), f32),
+            pltpu.VMEM((entries, modes_total, block), bf16),
             pltpu.VMEM((2, entries, nm, rows, block), f32),
             pltpu.VMEM((nm, entries, rows, block), f32),
             pltpu.VMEM((nm, entries, rows, block), f32),
@@ -493,10 +539,10 @@
             pltpu.VMEM((2, nm, rows, width), f32),
             pltpu.VMEM((2, rows, slab * block), f32),
             pltpu.VMEM((2, rows, slab * block), f32),
-            pltpu.VMEM((3, 8, 128), f32),
-            pltpu.VMEM((nm, 8, 128), f32),
-            pltpu.VMEM((cells_y, 8, 128), f32),
-            pltpu.VMEM((cells_z, 8, 128), f32),
+            pltpu.VMEM((3, 3, 8, 128), f32),
+            pltpu.VMEM((3, nm, 8, 128), f32),
+            pltpu.VMEM((3, cells_y, 8, 128), f32),
+            pltpu.VMEM((3, cells_z, 8, 128), f32),
             dma((2, max(nm, cells_y), 2)),
             dma((2,)),
             dma((2, nm, 2)),
@@ -504,9 +550,9 @@
             dma((2, cells_z, cells_y, 2)),
             dma((2, 2, cells_z, 2)),
             dma((2, nm, 2)),
-            dma((nm, 2)),
-            dma((cells_y, 2)),
-            dma((cells_z, 2)),
+            dma((3, nm, 2)),
+            dma((3, cells_y, 2)),
+            dma((3, cells_z, 2)),
         ],
         compiler_params=pltpu.CompilerParams(
             collective_id=0, has_side_effects=True, vmem_limit_bytes=62 * 1024 * 1024

time: 107 us -> 126 us (1.18)
  Pallas kernels: 104 us -> 123 us
    pallas_call x1, Pallas kernels: 104 us -> 123 us  [body(): pl.pallas_call(functools.partial(kernel, dims), out_shape=[jax.ShapeDtype...]
where the time goes in v3:
time: 126 us
  Pallas kernels  123 us (98%)
  local copies, waits for them, and re-layouts  2.26 us (2%)
    pallas_call x1, Pallas kernels, body(): pl.pallas_call(functools.partial(kernel, dims), out_shape=[jax.ShapeDtype...  123 us

profile of v3, /device:TPU:1, one launch (start us, length us, event | category | flops | bytes accessed | tf_op | source)
XLA Modules:
  0.0 126.4 jit_solution(17439665384848752754)
XLA Ops:
  0.6 123.4 %shard_map.77 = (f32[16,2048]{1,0:T(8,128)}, f32[16,2048]{1,0:T(8,128)}) custom-call(s32[2,1,9]{2,1,0:T(1,128)} %bitcast.7, s32[2,9]{1,0:T(2,128)} %target_ref.1, f32[16,2048]{1,0:T(8,128)} %source_hbm.1, f32[9,128,128]{2,1,0:T(8,128)} %coupling_hbm.1, bf16[18,128,128]{2,1,0:T(8,128)(2,1)} %bitcast.5, bf16[18,128,128]{2,1,0:T(8,128)(2,1)} %bitcast.6), custom_call_target="tpu_custom_call" | custom-call | tf_op jit(solution)/shard_map/pallas_call | solution.py:510
  124.1 0.0 copy-start
  124.1 1.6 %copy.11 = f32[16,2048]{1,0:T(8,128)} copy(f32[16,2048]{1,0:T(8,128)} %get-tuple-element.4) | data formatting | bytes 262144
  125.7 0.0 copy-done
  125.7 0.7 copy.12
Async XLA Ops:
  124.1 1.6 %copy-start = (f32[16,2048]{1,0:T(8,128)S(1)}, f32[16,2048]{1,0:T(8,128)}, u32[]{:S(2)}) copy-start(f32[16,2048]{1,0:T(8,128)} %get-tuple-element.5) | copy-start | bytes 393220

commit v4 on v3

--- a/solution.py
+++ b/solution.py
@@ -225,14 +225,12 @@
                 preferred_element_type=jnp.float32,
             )
 
-        third = (terms + 2) // 3
-        for k in range(0, third):
-            mix(k)
+        half = terms // 2
         sum_second(at)
-        for k in range(third, min(terms, 2 * third)):
+        for k in range(0, half):
             mix(k)
         sum_third(at)
-        for k in range(min(terms, 2 * third), terms):
+        for k in range(half, terms):
             mix(k)
         return sum_end(at)
 
@@ -311,7 +309,7 @@
                 return tuple(total + jnp.where(label == t, tile, 0.0) for t, total in enumerate(totals))
 
             zero = jnp.zeros((rows, block), jnp.float32)
-            totals = list(lax.fori_loop(0, ny * nm, add, (zero,) * slab))
+            totals = list(lax.fori_loop(0, ny * nm, add, (zero,) * slab, unroll=4))
             d = turns[i]
             middle = nz // 2
             everything = slice(0, slab)

time: 126 us -> 125 us (level)
    pallas_call x1, Pallas kernels: 123 us -> 122 us  [body(): pl.pallas_call(functools.partial(kernel, dims), out_shape=[jax.ShapeDtype...]
where the time goes in v4:
time: 125 us
  Pallas kernels  122 us (98%)
  local copies, waits for them, and re-layouts  2.26 us (2%)
    pallas_call x1, Pallas kernels, body(): pl.pallas_call(functools.partial(kernel, dims), out_shape=[jax.ShapeDtype...  122 us

profile of v4, /device:TPU:1, one launch (start us, length us, event | category | flops | bytes accessed | tf_op | source)
XLA Modules:
  0.0 124.6 jit_solution(10514373734180709853)
XLA Ops:
  0.6 121.7 %shard_map.77 = (f32[16,2048]{1,0:T(8,128)}, f32[16,2048]{1,0:T(8,128)}) custom-call(s32[2,1,9]{2,1,0:T(1,128)} %bitcast.7, s32[2,9]{1,0:T(2,128)} %target_ref.1, f32[16,2048]{1,0:T(8,128)} %source_hbm.1, f32[9,128,128]{2,1,0:T(8,128)} %coupling_hbm.1, bf16[18,128,128]{2,1,0:T(8,128)(2,1)} %bitcast.5, bf16[18,128,128]{2,1,0:T(8,128)(2,1)} %bitcast.6), custom_call_target="tpu_custom_call" | custom-call | tf_op jit(solution)/shard_map/pallas_call | solution.py:508
  122.3 0.0 copy-start
  122.3 1.6 %copy.11 = f32[16,2048]{1,0:T(8,128)} copy(f32[16,2048]{1,0:T(8,128)} %get-tuple-element.4) | data formatting | bytes 262144
  123.9 0.0 copy-done
  123.9 0.7 copy.12
Async XLA Ops:
  122.3 1.6 %copy-start = (f32[16,2048]{1,0:T(8,128)S(1)}, f32[16,2048]{1,0:T(8,128)}, u32[]{:S(2)}) copy-start(f32[16,2048]{1,0:T(8,128)} %get-tuple-element.5) | copy-start | bytes 393220

commit v5 on v4

--- a/solution.py
+++ b/solution.py
@@ -226,7 +226,6 @@
             )
 
         half = terms // 2
-        sum_second(at)
         for k in range(0, half):
             mix(k)
         sum_third(at)
@@ -395,6 +394,7 @@
         send(table_out, tables_row.at[m], table_sems.at[0, d], x_id(d))
     tables_row[m] = table_out[...]
     loads[1].wait()
+    sum_second(0)
     for d in range(1, nm):
         arrive(tables_row.at[x_peer(nm - d)], table_sems.at[0, d], x_id(d))
     for d in range(1, ny):
@@ -425,6 +425,7 @@
     complete(0)
     sum_start(1, pack([dot_lanes(first, source_ref), dot_lanes(first, first)]))
     regroup_start(1, far_sum.at[0])
+    sum_second(1)
     far = regroup_end(1)
     sums = mix_and_sum(1, far + near_out[0].reshape(modes_total, width))
     h00 = sums[0:1] * shrink

time: 125 us -> 123 us (0.984)
  Pallas kernels: 122 us -> 120 us
    pallas_call x1, Pallas kernels: 122 us -> 120 us  [body(): pl.pallas_call(functools.partial(kernel, dims), out_shape=[jax.ShapeDtype...]
where the time goes in v5:
time: 123 us
  Pallas kernels  120 us (98%)
  local copies, waits for them, and re-layouts  2.26 us (2%)
    pallas_call x1, Pallas kernels, body(): pl.pallas_call(functools.partial(kernel, dims), out_shape=[jax.ShapeDtype...  120 us

profile of v5, /device:TPU:1, one launch (start us, length us, event | category | flops | bytes accessed | tf_op | source)
XLA Modules:
  0.0 123.1 jit_solution(17770250773635176578)
XLA Ops:
  0.6 120.2 %shard_map.77 = (f32[16,2048]{1,0:T(8,128)}, f32[16,2048]{1,0:T(8,128)}) custom-call(s32[2,1,9]{2,1,0:T(1,128)} %bitcast.7, s32[2,9]{1,0:T(2,128)} %target_ref.1, f32[16,2048]{1,0:T(8,128)} %source_hbm.1, f32[9,128,128]{2,1,0:T(8,128)} %coupling_hbm.1, bf16[18,128,128]{2,1,0:T(8,128)(2,1)} %bitcast.5, bf16[18,128,128]{2,1,0:T(8,128)(2,1)} %bitcast.6), custom_call_target="tpu_custom_call" | custom-call | tf_op jit(solution)/shard_map/pallas_call | solution.py:509
  120.8 0.0 copy-start
  120.8 1.6 %copy.11 = f32[16,2048]{1,0:T(8,128)} copy(f32[16,2048]{1,0:T(8,128)} %get-tuple-element.4) | data formatting | bytes 262144
  122.4 0.0 copy-done
  122.4 0.7 copy.12
Async XLA Ops:
  120.8 1.6 %copy-start = (f32[16,2048]{1,0:T(8,128)S(1)}, f32[16,2048]{1,0:T(8,128)}, u32[]{:S(2)}) copy-start(f32[16,2048]{1,0:T(8,128)} %get-tuple-element.5) | copy-start | bytes 393220
